TPU v7x, 32 devices: a whole 2x2x4 slice. The times are simulated.
32 devices in a mesh: gx: 8 (over z, y), gy: 4 (over x, core).
Axes of the slice: x: 2, y: 2, z: 4, core: 2. Of those that a mesh axis runs over, the one named last changes fastest.
Arguments:
- thermal_anomaly: float32 [8, 256, 2048], P(None, 'gx', 'gy'), may hold values from -6 to 6
- saltiness_anomaly: float32 [8, 256, 2048], P(None, 'gx', 'gy'), may hold values from -6 to 6
- zonal_current: float32 [8, 256, 2048], P(None, 'gx', 'gy'), may hold values from -3 to 3
- meridional_current: float32 [8, 256, 2048], P(None, 'gx', 'gy'), may hold values from -3 to 3
- vertical_diffusion: float32 [7, 256, 2048], P(None, 'gx', 'gy'), may hold values from 0.1 to 10
- submerged_layers: int32 [256, 2048], P('gx', 'gy'), may hold values from 0 to 8
- strip_position_table: int32 [16], replicated, may hold values from -1 to 11, as said below
Outputs:
- temperature_out: float32 [8, 256, 2048], P(None, 'gx', 'gy')
- salinity_out: float32 [8, 256, 2048], P(None, 'gx', 'gy')
- surface_height: float32 [256, 2048], P('gx', 'gy')
- block_height: float32 [256, 1536], P('gx', 'gy')
Inputs may be any that keep to these rules, and one draw needn't show every extreme that they name: `strip_position_table`: 4 bands hold -1; the others form one run of consecutive bands holding 0, 1, ..., 11 in order, and where the run begins is drawn anew.
All inputs are finite; a program needn't handle non-finite values.
Results may differ from a plain program's by a relative error of at most 0.0003.
Values sent between devices are 32-bit elements; how exact they have to be, the bound alone decides.
A program may use at most 64 MiB of HBM per device.

v0:
```python
import jax
import jax.numpy as jnp
from jax import lax
from jax.sharding import PartitionSpec as P

BY = 128
KB = 3
SWEEPS = 4
RB = 384


TIME_STEP = 0.2
MIX_HORIZ = 0.25
SALT_COEF = 0.8
HEAT_COEF = 0.6
SURFACE_TERM = 0.5
CENTER = 5.5
HALF_SPAN = 5.0


def padded_2(block, sides, width):
    for axis, dim in sides:
        count = lax.axis_size(axis)
        forward = [(i, i + 1) for i in range(count - 1)]
        forward.append((count - 1, 0))
        backward = [(target, source) for source, target in forward]
        low = lax.ppermute(
            lax.slice_in_dim(block, block.shape[dim] - width, None, axis=dim), axis, forward
        )
        high = lax.ppermute(lax.slice_in_dim(block, 0, width, axis=dim), axis, backward)
        block = jnp.concatenate([low, block, high], axis=dim)
    return block


def thickness(layered_planes):
    layer_indices = jnp.arange(layered_planes, dtype=jnp.float32)
    return 2.0 * (layer_indices + 1.0) / (layered_planes * (layered_planes + 1.0))


def column_mix(updated_tracer, coupling):
    layered_planes = len(updated_tracer)
    zeros_plane = jnp.zeros_like(coupling[0])
    below_coupling = [zeros_plane] + list(coupling)
    above_coupling = list(coupling) + [zeros_plane]
    ratios = []
    values = []
    for level_index in range(layered_planes):
        pivot_value = 1.0 + below_coupling[level_index] + above_coupling[level_index]
        right_side = updated_tracer[level_index]
        if level_index > 0:
            pivot_value = pivot_value - below_coupling[level_index] * ratios[level_index - 1]
            right_side = right_side + below_coupling[level_index] * values[level_index - 1]
        ratios.append(above_coupling[level_index] / pivot_value)
        values.append(right_side / pivot_value)
    result = [None] * layered_planes
    result[layered_planes - 1] = values[layered_planes - 1]
    for level_index in range(layered_planes - 2, -1, -1):
        result[level_index] = values[level_index] + ratios[level_index] * result[level_index + 1]
    return jnp.stack(result, axis=1)


def chebyshev(source, apply_operator):
    scaled = CENTER / HALF_SPAN
    height = jnp.zeros_like(source)
    residual = source
    direction = source / CENTER
    weight_now = 1.0 / scaled
    for sweep_index in range(SWEEPS):
        height = height + direction
        residual = residual - apply_operator(direction)
        if sweep_index + 1 < SWEEPS:
            weight_next = 1.0 / (2.0 * scaled - weight_now)
            direction = (
                weight_next * weight_now * direction + 2.0 * weight_next / HALF_SPAN * residual
            )
            weight_now = weight_next
    return height


def take_rows(collected, shard_rows, offset, first_row, row_count):
    length = shard_rows.shape[1]
    padded = jnp.pad(shard_rows, ((0, 0), (row_count, row_count)))
    window = lax.dynamic_slice_in_dim(padded, first_row + row_count, row_count, 1)
    row_index = first_row + jnp.arange(row_count, dtype=jnp.int32)
    inside = (row_index >= offset) & (row_index < offset + length)
    return jnp.where(inside[None, :], window, collected)


def corner_local(depth_ext, ocean_ext):
    return (
        ocean_ext[:-1, :-1]
        * ocean_ext[1:, :-1]
        * ocean_ext[:-1, 1:]
        * ocean_ext[1:, 1:]
        * (depth_ext[:-1, :-1] + depth_ext[1:, :-1] + depth_ext[:-1, 1:] + depth_ext[1:, 1:])
        * 0.25
    )


def spread_local(field_ext, corner, ocean_inner):
    anchor = field_ext[:-1, :-1]
    along_x = field_ext[1:, :-1]
    along_y = field_ext[:-1, 1:]
    across = field_ext[1:, 1:]
    to_anchor = corner * (
        0.5 * (anchor - along_x) + 0.5 * (anchor - along_y) + 0.25 * (anchor - across)
    )
    to_along_x = corner * (
        0.5 * (along_x - anchor) + 0.5 * (along_x - across) + 0.25 * (along_x - along_y)
    )
    to_along_y = corner * (
        0.5 * (along_y - anchor) + 0.5 * (along_y - across) + 0.25 * (along_y - along_x)
    )
    to_across = corner * (
        0.5 * (across - along_x) + 0.5 * (across - along_y) + 0.25 * (across - anchor)
    )
    spread = to_anchor[1:, 1:] + to_along_x[:-1, 1:] + to_along_y[1:, :-1] + to_across[:-1, :-1]
    return ocean_inner * (SURFACE_TERM * field_ext[1:-1, 1:-1] + spread)


def body(
    thermal_anomaly,
    saltiness_anomaly,
    zonal_current,
    meridional_current,
    vertical_diffusion,
    submerged_layers,
    strip_position_table,
):
    layered_planes = thermal_anomaly.shape[0]
    vertical_profiles = thermal_anomaly.shape[1]
    block_line_indices = thermal_anomaly.shape[2]
    lat_devices = lax.axis_size("gy")
    tile_index = lax.axis_index("gy")
    total_rows = block_line_indices * lat_devices
    band_ids = jnp.arange(strip_position_table.shape[0], dtype=jnp.int32)
    band_flags = (strip_position_table >= 0).astype(jnp.float32)
    first_band = jnp.sum(jnp.where(strip_position_table == 0, band_ids, 0))
    top_row = first_band * BY + lat_devices * RB - 1
    stacked = jnp.concatenate(
        [
            thermal_anomaly,
            saltiness_anomaly,
            zonal_current,
            meridional_current,
            submerged_layers.astype(jnp.float32)[None],
        ],
        axis=0,
    )
    extended = padded_2(stacked, (("gx", 1), ("gy", 2)), 1)
    tracer_part = extended[: 2 * layered_planes]
    floor_raw = extended[4 * layered_planes]
    east_ext = extended[2 * layered_planes : 3 * layered_planes]
    north_ext = extended[3 * layered_planes : 4 * layered_planes]
    row_index = (
        tile_index * block_line_indices - 1 + jnp.arange(block_line_indices + 2, dtype=jnp.int32)
    )
    inside = ((row_index >= 0) & (row_index < total_rows)).astype(jnp.float32)
    floor_ext = floor_raw * inside[None, :]
    layer_indices = jnp.arange(layered_planes, dtype=jnp.float32)
    wet_ext = (layer_indices[:, None, None] < floor_ext[None]).astype(jnp.float32)
    tracer_ext = jnp.stack(
        [tracer_part[:layered_planes], tracer_part[layered_planes : 2 * layered_planes]]
    )
    west_side = tracer_ext[..., :-1, 1:-1]
    east_side = tracer_ext[..., 1:, 1:-1]
    face_flux = (
        wet_ext[:, :-1, 1:-1]
        * wet_ext[:, 1:, 1:-1]
        * (
            east_ext[:, :-1, 1:-1] * (west_side + east_side) * 0.5
            - MIX_HORIZ * (east_side - west_side)
        )
    )
    south_side = tracer_ext[..., 1:-1, :-1]
    north_side = tracer_ext[..., 1:-1, 1:]
    lat_flux = (
        wet_ext[:, 1:-1, :-1]
        * wet_ext[:, 1:-1, 1:]
        * (
            north_ext[:, 1:-1, :-1] * (south_side + north_side) * 0.5
            - MIX_HORIZ * (north_side - south_side)
        )
    )
    change = face_flux[..., 1:, :] - face_flux[..., :-1, :] + lat_flux[..., 1:] - lat_flux[..., :-1]
    wet_mask = wet_ext[:, 1:-1, 1:-1]
    updated_tracer = wet_mask * (tracer_ext[..., 1:-1, 1:-1] - TIME_STEP * change)
    coupling = [
        TIME_STEP
        * vertical_diffusion[level_index]
        * wet_mask[level_index]
        * wet_mask[level_index + 1]
        for level_index in range(layered_planes - 1)
    ]
    mixed_columns = column_mix(
        [updated_tracer[:, level_index] for level_index in range(layered_planes)], coupling
    )
    thicknesses = thickness(layered_planes)
    depth_ext = jnp.sum(thicknesses[:, None, None] * wet_ext, axis=0)
    forcing = jnp.sum(
        thicknesses[:, None, None] * (SALT_COEF * mixed_columns[1] - HEAT_COEF * mixed_columns[0]),
        axis=0,
    )
    band_start = (first_band + (lat_devices - 1 - tile_index) * KB) * BY
    depth_strip = depth_ext[:, 1:-1]
    initial = (
        jnp.zeros((vertical_profiles, RB), jnp.float32),
        jnp.zeros((vertical_profiles + 2, RB + 2), jnp.float32),
    )
    offset = jnp.int32(0)
    natural_forcing = take_rows(
        initial[0], lax.all_gather(forcing, "gy", axis=1, tiled=True), offset, band_start, RB
    )
    natural_depth = take_rows(
        initial[1],
        lax.all_gather(depth_strip, "gy", axis=1, tiled=True),
        offset,
        band_start - 1,
        RB + 2,
    )
    band_forcing = natural_forcing[:, ::-1]
    band_depth = natural_depth[:, ::-1]
    row_index = band_start - 1 + jnp.arange(RB + 2, dtype=jnp.int32)
    band_index = jnp.floor_divide(row_index, BY)
    matches = (band_index[:, None] == band_ids[None, :]).astype(jnp.float32)
    band_ocean = (band_depth > 0.0).astype(jnp.float32) * jnp.sum(
        matches * band_flags[None, :], axis=1
    )[::-1][None, :]
    band_inner = band_ocean[1:-1, 1:-1]
    band_corner = corner_local(band_depth, band_ocean)

    def band_operator(surface_field):
        field_ext = padded_2(surface_field, (("gx", 0), ("gy", 1)), 1)
        return spread_local(field_ext, band_corner, band_inner)

    block_out = chebyshev(band_inner * band_forcing, band_operator)
    back_row = top_row - (tile_index + 1) * block_line_indices + 1
    reversed_surface = take_rows(
        jnp.zeros((vertical_profiles, block_line_indices), jnp.float32),
        lax.all_gather(block_out, "gy", axis=1, tiled=True),
        jnp.int32(0),
        back_row,
        block_line_indices,
    )
    surface = reversed_surface[:, ::-1]
    return (mixed_columns[0], mixed_columns[1], surface, block_out)


def solution(mesh):
    placed = (
        P(None, "gx", "gy"),
        P(None, "gx", "gy"),
        P(None, "gx", "gy"),
        P(None, "gx", "gy"),
        P(None, "gx", "gy"),
        P("gx", "gy"),
        P(),
    )
    return jax.shard_map(
        body,
        mesh=mesh,
        in_specs=placed,
        out_specs=(P(None, "gx", "gy"), P(None, "gx", "gy"), P("gx", "gy"), P("gx", "gy")),
        check_vma=False,
    )
```

profile of v0, /device:TPU:0, one launch (start us, length us, event | category | flops | bytes accessed | tf_op | source)
XLA Modules:
  0.0 85.9 jit_solution(8542441219765018717)
XLA Ops:
  0.7 1.2 %constant_dynamic-update-slice_fusion.3 = f32[33,32,512]{2,1,0:T(8,128)S(1)} fusion(f32[8,32,512]{2,1,0:T(8,128)} %param.7), kind=kLoop, calls=%fused_computation.229 | loop fusion | bytes 1048576
  2.9 3.0 %collective-permute-start = (f32[33,1,512]{2,1,0:T(1,128)S(1)}, f32[33,1,512]{2,1,0:T(1,128)S(1)}, u32[]{:S(2)}, u32[]{:S(2)}) collective-permute-start(f32[33,1,512]{2,1,0:T(1,128)S(1)} %get-tuple-element.46), channel_id=1, source_target_pairs={{0,4},{4,8},{8,12},{12,16},{16,20},{20,24},{24,28},{28,0},{1,5},{5... | collective-permute-start | bytes 202760 | tf_op jit(solution)/shard_map/ppermute | solution.py:27
  5.9 3.1 %collective-permute-start.1 = (f32[33,1,512]{2,1,0:T(1,128)S(1)}, f32[33,1,512]{2,1,0:T(1,128)}, u32[]{:S(2)}, u32[]{:S(2)}) collective-permute-start(f32[33,1,512]{2,1,0:T(1,128)S(1)} %get-tuple-element.47), channel_id=1, source_target_pairs={{4,0},{8,4},{12,8},{16,12},{20,16},{24,20},{28,24},{0,28},{5,1},{9... | collective-permute-start | bytes 202760 | tf_op jit(solution)/shard_map/ppermute | solution.py:30
  14.0 1.1 %pad_maximum_fusion.7 = (f32[33,34,1]{2,1,0:T(8,128)S(1)}, f32[33,34,1]{2,1,0:T(8,128)S(1)}) fusion(f32[33,1,512]{2,1,0:T(1,128)} %collective-permute-done.1, f32[33,32,512]{2,1,0:T(8,128)S(1)} %bitcast_dynamic-update-slice_fusion, f32[33,1,512]{2,1,0:T(1,128)} %copy-done.8), kind=kLoop, calls=%fused_computation.32 | loop fusion | flops 4488 | bytes 2306832 | tf_op jit(solution)/shard_map/slice | solution.py:28
  16.5 1.7 %pad_maximum_fusion.11 = f32[8,33,512]{2,1,0:T(8,128)} fusion(f32[33,32,512]{2,1,0:T(8,128)S(1)} %bitcast_dynamic-update-slice_fusion, f32[33,1,512]{2,1,0:T(1,128)} %copy-done.8), kind=kLoop, calls=%fused_computation.37 | loop fusion | flops 135168 | bytes 2770944 | tf_op jit(solution)/shard_map/concatenate | solution.py:31
  18.1 1.5 %collective-permute-done.2 = f32[33,34,1]{1,2,0:T(1,128)S(1)} collective-permute-done((f32[33,34,1]{1,2,0:T(1,128)S(1)}, f32[33,34,1]{1,2,0:T(1,128)S(1)}, u32[]{:S(2)}, u32[]{:S(2)}) %collective-permute-start.2) | collective-permute-done | bytes 4520 | tf_op jit(solution)/shard_map/ppermute | solution.py:27
  22.6 1.0 %slice.432 = f32[8,32,512]{2,1,0:T(8,128)} slice(f32[8,34,514]{2,1,0:T(8,128)S(1)} %fusion.8), slice={[0:8], [1:33], [1:513]} | slice | bytes 1048576 | tf_op jit(solution)/shard_map/slice | solution.py:186
  23.6 1.1 %slice_multiply_fusion = f32[8,32,513]{2,1,0:T(8,128)} fusion(f32[8,34,514]{2,1,0:T(8,128)S(1)} %fusion.8), kind=kLoop, calls=%fused_computation.36 | loop fusion | flops 131328 | bytes 1575936 | tf_op jit(solution)/shard_map/mul | solution.py:178
  24.7 1.2 %slice_multiply_fusion.1 = f32[8,33,512]{2,1,0:T(8,128)} fusion(f32[8,34,514]{2,1,0:T(8,128)S(1)} %fusion.8), kind=kLoop, calls=%fused_computation.38 | loop fusion | flops 135168 | bytes 1622016 | tf_op jit(solution)/shard_map/mul | solution.py:168
  26.2 6.0 %all_gather.9 = f32[34,2048]{1,0:T(8,128)S(1)} all-gather(f32[34,512]{1,0:T(8,128)S(1)} %slice.467), channel_id=1, replica_groups=mesh['gx'=8,'gy'=4] {'gy'}, dimensions={1}, use_global_device_ids=true | all-gather | bytes 348160 | tf_op jit(solution)/shard_map/all_gather | solution.py:216
  32.2 1.5 %reverse.4 = f32[34,512]{1,0:T(8,128)} reverse(f32[34,512]{1,0:T(8,128)S(1)} %bitcast.54), dimensions={1} | reverse | bytes 139264
  35.1 1.6 %fusion.7 = (f32[1,8,34,514]{3,2,1,0:T(8,128)S(1)}, f32[1,8,34,514]{3,2,1,0:T(8,128)S(1)}) fusion(f32[33,34,1]{2,1,0:T(8,128)S(1)} %copy-done.3, f32[33,34,1]{2,1,0:T(8,128)S(1)} %copy-done.1, f32[33,1,512]{2,1,0:T(1,128)} %collective-permute-done.1, f32[33,32,512]{2,1,0:T(8,128)S(1)} %bitcast_dynamic-update-slice_fusion, f32[33,1,512]{2,1,0:T(1,128)S(1)} %copy-done.9), kind=kLoop, calls=%fused_computation.22 | loop fusion | flops 1118464 | bytes 3425296 | tf_op jit(solution)/shard_map/stack | solution.py:162
  41.0 1.2 %multiply_reduce_fusion = (f32[32,512]{1,0:T(8,128)S(1)}, f32[8,32,512]{2,1,0:T(8,128)}, f32[8,32,512]{2,1,0:T(8,128)}) fusion(f32[8]{0:T(128)S(1)} %copy-done.19, f32[2,8,32,512]{3,2,1,0:T(8,128)S(1)} %constant_dynamic-update-slice_fusion.4), kind=kLoop, calls=%fused_computation.41 | loop fusion | flops 638976 | bytes 2162720 | tf_op jit(solution)/shard_map/reduce_sum | solution.py:200
  42.1 5.8 %all_gather.10 = f32[32,2048]{1,0:T(8,128)S(1)} all-gather(f32[32,512]{1,0:T(8,128)S(1)} %get-tuple-element.18), channel_id=1, replica_groups=mesh['gx'=8,'gy'=4] {'gy'}, dimensions={1}, use_global_device_ids=true | all-gather | bytes 327680 | tf_op jit(solution)/shard_map/all_gather | solution.py:212
  48.5 4.7 %collective-permute-start.5 = (f32[1,384]{1,0:T(1,128)S(1)}, f32[1,384]{1,0:T(1,128)S(1)}, u32[]{:S(2)}, u32[]{:S(2)}) collective-permute-start(f32[1,384]{1,0:T(1,128)S(1)} %get-tuple-element.88), channel_id=1, source_target_pairs={{4,0},{8,4},{12,8},{16,12},{20,16},{24,20},{28,24},{0,28},{5,1},{9... | collective-permute-start | bytes 4616 | tf_op jit(solution)/shard_map/ppermute | solution.py:30
  55.6 1.0 %collective-permute-done.7 = f32[34,1]{1,0:T(8,128)S(1)} collective-permute-done((f32[34,1]{1,0:T(8,128)S(1)}, f32[34,1]{1,0:T(8,128)S(1)}, u32[]{:S(2)}, u32[]{:S(2)}) %collective-permute-start.7) | collective-permute-done | bytes 168 | tf_op jit(solution)/shard_map/ppermute | solution.py:30
  56.6 1.7 %collective-permute-done.6 = f32[34,1]{1,0:T(8,128)S(1)} collective-permute-done((f32[34,1]{1,0:T(8,128)S(1)}, f32[34,1]{1,0:T(8,128)S(1)}, u32[]{:S(2)}, u32[]{:S(2)}) %collective-permute-start.6) | collective-permute-done | bytes 168 | tf_op jit(solution)/shard_map/ppermute | solution.py:27
  58.7 4.7 %collective-permute-start.9 = (f32[1,384]{1,0:T(1,128)S(1)}, f32[1,384]{1,0:T(1,128)S(1)}, u32[]{:S(2)}, u32[]{:S(2)}) collective-permute-start(f32[1,384]{1,0:T(1,128)S(1)} %get-tuple-element.86), channel_id=1, source_target_pairs={{4,0},{8,4},{12,8},{16,12},{20,16},{24,20},{28,24},{0,28},{5,1},{9... | collective-permute-start | bytes 4616 | tf_op jit(solution)/shard_map/ppermute | solution.py:30
  66.6 1.8 %collective-permute-done.10 = f32[34,1]{1,0:T(8,128)S(1)} collective-permute-done((f32[34,1]{1,0:T(8,128)S(1)}, f32[34,1]{1,0:T(8,128)S(1)}, u32[]{:S(2)}, u32[]{:S(2)}) %collective-permute-start.10) | collective-permute-done | bytes 168 | tf_op jit(solution)/shard_map/ppermute | solution.py:27
  68.8 4.8 %collective-permute-start.13 = (f32[1,384]{1,0:T(1,128)S(1)}, f32[1,384]{1,0:T(1,128)S(1)}, u32[]{:S(2)}, u32[]{:S(2)}) collective-permute-start(f32[1,384]{1,0:T(1,128)S(1)} %get-tuple-element.84), channel_id=1, source_target_pairs={{4,0},{8,4},{12,8},{16,12},{20,16},{24,20},{28,24},{0,28},{5,1},{9... | collective-permute-start | bytes 4616 | tf_op jit(solution)/shard_map/ppermute | solution.py:30
  73.6 1.5 %collective-permute-done.12 = f32[1,384]{1,0:T(1,128)S(1)} collective-permute-done((f32[1,384]{1,0:T(1,128)S(1)}, f32[1,384]{1,0:T(1,128)S(1)}, u32[]{:S(2)}, u32[]{:S(2)}) %collective-permute-start.12) | collective-permute-done | bytes 1568 | tf_op jit(solution)/shard_map/ppermute | solution.py:27
  76.6 1.8 %collective-permute-done.14 = f32[34,1]{1,0:T(8,128)S(1)} collective-permute-done((f32[34,1]{1,0:T(8,128)S(1)}, f32[34,1]{1,0:T(8,128)S(1)}, u32[]{:S(2)}, u32[]{:S(2)}) %collective-permute-start.14) | collective-permute-done | bytes 168 | tf_op jit(solution)/shard_map/ppermute | solution.py:27
  78.8 5.6 %all_gather.11 = f32[32,1536]{1,0:T(8,128)S(1)} all-gather(f32[32,384]{1,0:T(8,128)S(1)} %fusion.34), channel_id=1, replica_groups=mesh['gx'=8,'gy'=4] {'gy'}, dimensions={1}, use_global_device_ids=true | all-gather | bytes 245760 | tf_op jit(solution)/shard_map/all_gather | solution.py:240
  84.5 1.5 %rev.15 = f32[32,512]{1,0:T(8,128)} reverse(f32[32,512]{1,0:T(8,128)S(1)} %fusion.21), dimensions={1} | reverse | bytes 131072 | tf_op jit(solution)/shard_map/rev | solution.py:245
  (139 shorter events, 23.5 us)
Async XLA Ops:
  2.0 7.6 %copy-start.22 = (s32[16]{0:T(128)S(1)}, s32[16]{0:T(128)}, u32[]{:S(2)}) copy-start(s32[16]{0:T(128)} %param.13) | copy-start | bytes 196
  2.9 10.5 %collective-permute-start = (f32[33,1,512]{2,1,0:T(1,128)S(1)}, f32[33,1,512]{2,1,0:T(1,128)S(1)}, u32[]{:S(2)}, u32[]{:S(2)}) collective-permute-start(f32[33,1,512]{2,1,0:T(1,128)S(1)} %get-tuple-element.46), channel_id=1, source_target_pairs={{0,4},{4,8},{8,12},{12,16},{16,20},{20,24},{24,28},{28,0},{1,5},{5... | collective-permute-start | bytes 202760 | tf_op jit(solution)/shard_map/ppermute | solution.py:27
  5.9 8.1 %collective-permute-start.1 = (f32[33,1,512]{2,1,0:T(1,128)S(1)}, f32[33,1,512]{2,1,0:T(1,128)}, u32[]{:S(2)}, u32[]{:S(2)}) collective-permute-start(f32[33,1,512]{2,1,0:T(1,128)S(1)} %get-tuple-element.47), channel_id=1, source_target_pairs={{4,0},{8,4},{12,8},{16,12},{20,16},{24,20},{28,24},{0,28},{5,1},{9... | collective-permute-start | bytes 202760 | tf_op jit(solution)/shard_map/ppermute | solution.py:30
  15.8 4.2 %collective-permute-start.3 = (f32[33,34,1]{1,2,0:T(1,128)S(1)}, f32[33,34,1]{1,2,0:T(1,128)S(1)}, u32[]{:S(2)}, u32[]{:S(2)}) collective-permute-start(f32[33,34,1]{1,2,0:T(1,128)S(1)} %copy.134), channel_id=1, source_target_pairs={{1,0},{2,1},{3,2},{0,3},{5,4},{6,5},{7,6},{4,7},{9,8},{10,9},{11,1... | collective-permute-start | bytes 13472 | tf_op jit(solution)/shard_map/ppermute | solution.py:30
  16.5 3.2 %collective-permute-start.2 = (f32[33,34,1]{1,2,0:T(1,128)S(1)}, f32[33,34,1]{1,2,0:T(1,128)S(1)}, u32[]{:S(2)}, u32[]{:S(2)}) collective-permute-start(f32[33,34,1]{1,2,0:T(1,128)S(1)} %copy.133), channel_id=1, source_target_pairs={{0,1},{1,2},{2,3},{3,0},{4,5},{5,6},{6,7},{7,4},{8,9},{9,10},{10,1... | collective-permute-start | bytes 13472 | tf_op jit(solution)/shard_map/ppermute | solution.py:27
  19.6 2.1 %copy-start.17 = (f32[514]{0:T(1024)S(1)}, f32[514]{0:T(1024)}, u32[]{:S(2)}) copy-start(f32[514]{0:T(1024)} %fusion.109) | copy-start | bytes 6172
  24.7 7.5 %copy-start.21 = (pred[386]{0:T(512)(128)(4,1)S(1)}, pred[386]{0:T(512)(128)(4,1)}, u32[]{:S(2)}) copy-start(pred[386]{0:T(512)(128)(4,1)} %fusion.120) | copy-start | bytes 1162
  24.7 9.0 %copy-start.13 = (f32[7,32,512]{2,1,0:T(8,128)S(1)}, f32[7,32,512]{2,1,0:T(8,128)}, u32[]{:S(2)}) copy-start(f32[7,32,512]{2,1,0:T(8,128)} %param.11) | copy-start | bytes 1376260
  40.9 7.1 %copy-start.20 = (pred[384]{0:T(512)(128)(4,1)S(1)}, pred[384]{0:T(512)(128)(4,1)}, u32[]{:S(2)}) copy-start(pred[384]{0:T(512)(128)(4,1)} %fusion.121) | copy-start | bytes 1156
  40.9 7.3 %copy-start.14 = (f32[34,512]{1,0:T(8,128)S(1)}, f32[34,512]{1,0:T(8,128)}, u32[]{:S(2)}) copy-start(f32[34,512]{1,0:T(8,128)} %reverse.4) | copy-start | bytes 208900
  41.0 7.3 %copy-start.18 = (f32[386]{0:T(512)S(1)}, f32[386]{0:T(512)}, u32[]{:S(2)}) copy-start(f32[386]{0:T(512)} %slice.981) | copy-start | bytes 4636
  48.5 6.3 %collective-permute-start.4 = (f32[1,384]{1,0:T(1,128)S(1)}, f32[1,384]{1,0:T(1,128)S(1)}, u32[]{:S(2)}, u32[]{:S(2)}) collective-permute-start(f32[1,384]{1,0:T(1,128)S(1)} %get-tuple-element.87), channel_id=1, source_target_pairs={{0,4},{4,8},{8,12},{12,16},{16,20},{20,24},{24,28},{28,0},{1,5},{5... | collective-permute-start | bytes 4616 | tf_op jit(solution)/shard_map/ppermute | solution.py:27
  48.5 6.3 %collective-permute-start.5 = (f32[1,384]{1,0:T(1,128)S(1)}, f32[1,384]{1,0:T(1,128)S(1)}, u32[]{:S(2)}, u32[]{:S(2)}) collective-permute-start(f32[1,384]{1,0:T(1,128)S(1)} %get-tuple-element.88), channel_id=1, source_target_pairs={{4,0},{8,4},{12,8},{16,12},{20,16},{24,20},{28,24},{0,28},{5,1},{9... | collective-permute-start | bytes 4616 | tf_op jit(solution)/shard_map/ppermute | solution.py:30
  54.9 1.7 %collective-permute-start.7 = (f32[34,1]{1,0:T(8,128)S(1)}, f32[34,1]{1,0:T(8,128)S(1)}, u32[]{:S(2)}, u32[]{:S(2)}) collective-permute-start(f32[34,1]{1,0:T(8,128)S(1)} %get-tuple-element.81), channel_id=1, source_target_pairs={{1,0},{2,1},{3,2},{0,3},{5,4},{6,5},{7,6},{4,7},{9,8},{10,9},{11,1... | collective-permute-start | bytes 416 | tf_op jit(solution)/shard_map/ppermute | solution.py:30
  55.1 3.2 %collective-permute-start.6 = (f32[34,1]{1,0:T(8,128)S(1)}, f32[34,1]{1,0:T(8,128)S(1)}, u32[]{:S(2)}, u32[]{:S(2)}) collective-permute-start(f32[34,1]{1,0:T(8,128)S(1)} %get-tuple-element.82), channel_id=1, source_target_pairs={{0,1},{1,2},{2,3},{3,0},{4,5},{5,6},{6,7},{7,4},{8,9},{9,10},{10,1... | collective-permute-start | bytes 416 | tf_op jit(solution)/shard_map/ppermute | solution.py:27
  58.7 6.3 %collective-permute-start.8 = (f32[1,384]{1,0:T(1,128)S(1)}, f32[1,384]{1,0:T(1,128)S(1)}, u32[]{:S(2)}, u32[]{:S(2)}) collective-permute-start(f32[1,384]{1,0:T(1,128)S(1)} %get-tuple-element.85), channel_id=1, source_target_pairs={{0,4},{4,8},{8,12},{12,16},{16,20},{20,24},{24,28},{28,0},{1,5},{5... | collective-permute-start | bytes 4616 | tf_op jit(solution)/shard_map/ppermute | solution.py:27
  58.7 6.3 %collective-permute-start.9 = (f32[1,384]{1,0:T(1,128)S(1)}, f32[1,384]{1,0:T(1,128)S(1)}, u32[]{:S(2)}, u32[]{:S(2)}) collective-permute-start(f32[1,384]{1,0:T(1,128)S(1)} %get-tuple-element.86), channel_id=1, source_target_pairs={{4,0},{8,4},{12,8},{16,12},{20,16},{24,20},{28,24},{0,28},{5,1},{9... | collective-permute-start | bytes 4616 | tf_op jit(solution)/shard_map/ppermute | solution.py:30
  65.1 1.5 %collective-permute-start.11 = (f32[34,1]{1,0:T(8,128)S(1)}, f32[34,1]{1,0:T(8,128)S(1)}, u32[]{:S(2)}, u32[]{:S(2)}) collective-permute-start(f32[34,1]{1,0:T(8,128)S(1)} %get-tuple-element.77), channel_id=1, source_target_pairs={{1,0},{2,1},{3,2},{0,3},{5,4},{6,5},{7,6},{4,7},{9,8},{10,9},{11,1... | collective-permute-start | bytes 416 | tf_op jit(solution)/shard_map/ppermute | solution.py:30
  65.1 3.3 %collective-permute-start.10 = (f32[34,1]{1,0:T(8,128)S(1)}, f32[34,1]{1,0:T(8,128)S(1)}, u32[]{:S(2)}, u32[]{:S(2)}) collective-permute-start(f32[34,1]{1,0:T(8,128)S(1)} %get-tuple-element.78), channel_id=1, source_target_pairs={{0,1},{1,2},{2,3},{3,0},{4,5},{5,6},{6,7},{7,4},{8,9},{9,10},{10,1... | collective-permute-start | bytes 416 | tf_op jit(solution)/shard_map/ppermute | solution.py:27
  68.7 6.3 %collective-permute-start.12 = (f32[1,384]{1,0:T(1,128)S(1)}, f32[1,384]{1,0:T(1,128)S(1)}, u32[]{:S(2)}, u32[]{:S(2)}) collective-permute-start(f32[1,384]{1,0:T(1,128)S(1)} %get-tuple-element.83), channel_id=1, source_target_pairs={{0,4},{4,8},{8,12},{12,16},{16,20},{20,24},{24,28},{28,0},{1,5},{5... | collective-permute-start | bytes 4616 | tf_op jit(solution)/shard_map/ppermute | solution.py:27
  68.8 6.3 %collective-permute-start.13 = (f32[1,384]{1,0:T(1,128)S(1)}, f32[1,384]{1,0:T(1,128)S(1)}, u32[]{:S(2)}, u32[]{:S(2)}) collective-permute-start(f32[1,384]{1,0:T(1,128)S(1)} %get-tuple-element.84), channel_id=1, source_target_pairs={{4,0},{8,4},{12,8},{16,12},{20,16},{24,20},{28,24},{0,28},{5,1},{9... | collective-permute-start | bytes 4616 | tf_op jit(solution)/shard_map/ppermute | solution.py:30
  75.2 1.5 %collective-permute-start.15 = (f32[34,1]{1,0:T(8,128)S(1)}, f32[34,1]{1,0:T(8,128)S(1)}, u32[]{:S(2)}, u32[]{:S(2)}) collective-permute-start(f32[34,1]{1,0:T(8,128)S(1)} %get-tuple-element.73), channel_id=1, source_target_pairs={{1,0},{2,1},{3,2},{0,3},{5,4},{6,5},{7,6},{4,7},{9,8},{10,9},{11,1... | collective-permute-start | bytes 416 | tf_op jit(solution)/shard_map/ppermute | solution.py:30
  75.2 3.3 %collective-permute-start.14 = (f32[34,1]{1,0:T(8,128)S(1)}, f32[34,1]{1,0:T(8,128)S(1)}, u32[]{:S(2)}, u32[]{:S(2)}) collective-permute-start(f32[34,1]{1,0:T(8,128)S(1)} %get-tuple-element.74), channel_id=1, source_target_pairs={{0,1},{1,2},{2,3},{3,0},{4,5},{5,6},{6,7},{7,4},{8,9},{9,10},{10,1... | collective-permute-start | bytes 416 | tf_op jit(solution)/shard_map/ppermute | solution.py:27
  78.8 7.1 %copy-start.15 = (f32[32,384]{1,0:T(8,128)}, f32[32,384]{1,0:T(8,128)S(1)}, u32[]{:S(2)}) copy-start(f32[32,384]{1,0:T(8,128)S(1)} %fusion.34) | copy-start | bytes 147460
  (15 other events, 17.7 us)
where the time goes:
time: 86.4 us; the launch traced here: 85.9 us
  starting transfers between devices  22.7 us (26%)
  blocking collectives  17.4 us (20%)
  other arithmetic  17.1 us (20%)
  local copies, waits for them, and re-layouts  13.9 us (16%)
  waiting for transfers between devices  12.4 us (14%)
  between operations  2.33 us (3%)
    ppermute x8, starting transfers between devices, padded_2(): lax.ppermute(lax.slice_in_dim(block, 0, width, axis=dim), axis, backward)  18.2 us
    unnamed x62, local copies, waits for them, and re-layouts  10.1 us
    ppermute x8, waiting for transfers between devices, padded_2(): lax.ppermute(lax.slice_in_dim(block, block.shape[dim] - width, None, axis...  9.44 us
    all_gather x1, blocking collectives, body(): lax.all_gather(depth_strip, 'gy', axis=1, tiled=True)  5.97 us
    all_gather x1, blocking collectives, body(): lax.all_gather(forcing, 'gy', axis=1, tiled=True)  5.85 us
    all_gather x1, blocking collectives, body(): lax.all_gather(block_out, 'gy', axis=1, tiled=True)  5.61 us
    ppermute x8, starting transfers between devices, padded_2(): lax.ppermute(lax.slice_in_dim(block, block.shape[dim] - width, None, axis...  4.51 us
    ppermute x8, waiting for transfers between devices, padded_2(): lax.ppermute(lax.slice_in_dim(block, 0, width, axis=dim), axis, backward)  2.95 us
  transfers between devices with their start and end apart: 16, of which 10 were waited for; matrix products, arithmetic and copies ran while one was open for 9% of the time, Pallas kernels for 0%

commit v1 on v0

v1 whole, which is shorter than its diff:
```python
import functools

import jax
import jax.numpy as jnp
from jax import lax
from jax.experimental import pallas as pl
from jax.experimental.pallas import tpu as pltpu
from jax.sharding import PartitionSpec as P

BY = 128
KB = 3
SWEEPS = 4
RB = KB * BY

TIME_STEP = 0.2
MIX_HORIZ = 0.25
SALT_COEF = 0.8
HEAT_COEF = 0.6
SURFACE_TERM = 0.5
CENTER = 5.5
HALF_SPAN = 5.0

MESH = pl.DeviceIdType.MESH
F32 = jnp.float32
CORNERS = ((1, 1), (1, -1), (-1, 1), (-1, -1))


def roll(x, shift, axis):
    return pltpu.roll(x, shift % x.shape[axis], axis)


def step_flux(current, here, there, mask):
    half = (TIME_STEP * 0.5) * current
    mixing = TIME_STEP * MIX_HORIZ
    low = jnp.where(mask, half + mixing, 0.0)
    high = jnp.where(mask, half - mixing, 0.0)
    return [low * h + high * t for h, t in zip(here, there)]


def reverse_lanes(x):
    lane = lax.broadcasted_iota(jnp.int32, x.shape, x.ndim - 1)
    for bit in range(7):
        s = 1 << bit
        x = jnp.where((lane & s) != 0, roll(x, s, x.ndim - 1), roll(x, -s, x.ndim - 1))
    return x


def kernel(
    nx, ny, table, t_hbm, s_hbm, u_hbm, v_hbm, k_hbm, l_hbm,
    t_out, s_out, h_out, b_out,
    tv, sv, uv, vv, kv, lv, lf, st, ss, inv, ratio,
    to_e, to_w, to_n, to_s, from_w, from_e, from_s, from_n, layer_c,
    src, src_w, src_e, src_s, src_n, src_c,
    bands, pool, height, block,
    in_sem, out_sem, send1, recv1, send2, recv2, send3, recv3,
):
    levels, nrow, nlane = t_hbm.shape
    tiles = nlane // BY
    reach = (ny + KB - 1) // KB + 1
    slots = ny + KB
    gx = lax.axis_index("gx")
    gy = lax.axis_index("gy")
    east, west = lax.rem(gx + 1, nx), lax.rem(gx + nx - 1, nx)
    north, south = lax.rem(gy + 1, ny), lax.rem(gy + ny - 1, ny)
    pick_x = {1: east, -1: west}
    pick_y = {1: north, -1: south}

    barrier = pltpu.get_barrier_semaphore()
    for x in (east, west):
        for y in (gy, north, south):
            pl.semaphore_signal(barrier, inc=1, device_id=(x, y), device_id_type=MESH)
    for hop in range(1, ny):
        pl.semaphore_signal(
            barrier, inc=1, device_id=(gx, lax.rem(gy + hop, ny)), device_id_type=MESH
        )

    loads = [
        pltpu.make_async_copy(a, b, in_sem.at[i])
        for i, (a, b) in enumerate(
            ((l_hbm, lv), (t_hbm, tv), (s_hbm, sv), (u_hbm, uv), (v_hbm, vv), (k_hbm, kv))
        )
    ]
    for copy in loads:
        copy.start()

    lane = lax.broadcasted_iota(jnp.int32, (nrow, BY), 1)
    loads[0].wait()
    lf[...] = lv[...].astype(F32)
    for copy in loads[1:5]:
        copy.wait()

    for k in range(levels):
        to_e[k : k + 1, :] = tv[k, nrow - 1 : nrow, :]
        to_e[levels + k : levels + k + 1, :] = sv[k, nrow - 1 : nrow, :]
        to_e[2 * levels + k : 2 * levels + k + 1, :] = uv[k, nrow - 1 : nrow, :]
        to_w[k : k + 1, :] = tv[k, 0:1, :]
        to_w[levels + k : levels + k + 1, :] = sv[k, 0:1, :]
    to_e[3 * levels :, :] = lf[nrow - 8 :, :]
    to_w[2 * levels :, :] = lf[:8, :]
    packed = jnp.zeros((nrow, BY), F32)
    for i, ref in enumerate((tv, sv, vv)):
        for k in range(levels):
            packed = jnp.where(lane == i * levels + k, ref[k, :, nlane - 1 : nlane], packed)
    to_n[:, :BY] = packed
    to_n[:, BY:] = lf[:, nlane - BY :]
    packed = jnp.zeros((nrow, BY), F32)
    for i, ref in enumerate((tv, sv)):
        for k in range(levels):
            packed = jnp.where(lane == i * levels + k, ref[k, :, 0:1], packed)
    to_s[:, :BY] = packed
    to_s[:, BY:] = lf[:, :BY]

    def corner_of(ref, dx, dy):
        return ref.at[
            pl.ds(nrow - 8 if dx > 0 else 0, 8), pl.ds(nlane - BY if dy > 0 else 0, BY)
        ]

    def remote(source, target, sends, recvs, i, device):
        return pltpu.make_async_remote_copy(
            src_ref=source, dst_ref=target, send_sem=sends.at[i], recv_sem=recvs.at[i],
            device_id=device, device_id_type=MESH,
        )

    pl.semaphore_wait(barrier, 6 + ny - 1)
    first = [
        remote(to_e, from_w, send1, recv1, 0, (east, gy)),
        remote(to_w, from_e, send1, recv1, 1, (west, gy)),
        remote(to_n, from_s, send1, recv1, 2, (gx, north)),
        remote(to_s, from_n, send1, recv1, 3, (gx, south)),
    ] + [
        remote(corner_of(lf, dx, dy), layer_c.at[c], send1, recv1, 4 + c, (pick_x[dx], pick_y[dy]))
        for c, (dx, dy) in enumerate(CORNERS)
    ]
    for copy in first:
        copy.start()

    layers = lf[...]
    row_id = lax.broadcasted_iota(jnp.int32, (nrow, nlane), 0)
    lane_id = lax.broadcasted_iota(jnp.int32, (nrow, nlane), 1)
    least_e = jnp.where(row_id == nrow - 1, 0.0, jnp.minimum(layers, roll(layers, -1, 0)))
    least_n = jnp.where(lane_id == nlane - 1, 0.0, jnp.minimum(layers, roll(layers, -1, 1)))
    for k in range(levels):
        wet = layers > k
        tracers = [tv[k], sv[k]]
        fe = step_flux(uv[k], tracers, [roll(c, -1, 0) for c in tracers], least_e > k)
        fn = step_flux(vv[k], tracers, [roll(c, -1, 1) for c in tracers], least_n > k)
        for ref, c, e, n in zip((st, ss), tracers, fe, fn):
            ref[k] = jnp.where(wet, c, 0.0) - (e - roll(e, 1, 0)) - (n - roll(n, 1, 1))
    loads[5].wait()
    for l in range(tiles):
        part = slice(l * BY, (l + 1) * BY)
        lay = lf[:, part]
        below = jnp.zeros((nrow, BY), F32)
        last = below
        for k in range(levels):
            pivot = 1.0 + below
            if k < levels - 1:
                above = jnp.where(lay > k + 1, TIME_STEP * kv[k, :, part], 0.0)
                kv[k, :, part] = above
                pivot = pivot + above
            if k > 0:
                pivot = pivot - below * last
            one = 1.0 / pivot
            inv[k, :, part] = one
            if k < levels - 1:
                last = above * one
                ratio[k, :, part] = last
                below = above

    for copy in first:
        copy.wait_recv()
    ends_n = jnp.where(gy == ny - 1, 0.0, 1.0).astype(F32)
    ends_s = jnp.where(gy == 0, 0.0, 1.0).astype(F32)

    level_row = lax.broadcasted_iota(jnp.int32, (levels, nlane), 0).astype(F32)
    face = step_flux(
        to_e[2 * levels : 3 * levels, :],
        [to_e[:levels, :], to_e[levels : 2 * levels, :]],
        [from_e[:levels, :], from_e[levels : 2 * levels, :]],
        jnp.minimum(lf[nrow - 1 : nrow, :], from_e[2 * levels : 2 * levels + 1, :]) > level_row,
    )
    for ref, flux in zip((st, ss), face):
        for k in range(levels):
            ref[k, nrow - 1 : nrow, :] = ref[k, nrow - 1 : nrow, :] - flux[k : k + 1, :]
    face = step_flux(
        from_w[2 * levels : 3 * levels, :],
        [from_w[:levels, :], from_w[levels : 2 * levels, :]],
        [to_w[:levels, :], to_w[levels : 2 * levels, :]],
        jnp.minimum(lf[0:1, :], from_w[3 * levels + 7 : 3 * levels + 8, :]) > level_row,
    )
    for ref, flux in zip((st, ss), face):
        for k in range(levels):
            ref[k, 0:1, :] = ref[k, 0:1, :] + flux[k : k + 1, :]
    level_lane = (lane & (levels - 1)).astype(F32)

    def lane_face(here, there, least):
        held = here[:, :BY]
        current = jnp.where(
            lane < levels, roll(held, -2 * levels, 1), roll(held, -levels, 1)
        )
        return step_flux(current, [held], [there[:, :BY]], least > level_lane)[0]

    face_n = lane_face(
        to_n, from_n, jnp.minimum(lf[:, nlane - 1 : nlane], from_n[:, BY : BY + 1] * ends_n)
    )
    face_s = lane_face(
        from_s, to_s, jnp.minimum(lf[:, 0:1], from_s[:, 2 * BY - 1 : 2 * BY] * ends_s)
    )

    thick = [2.0 * (k + 1.0) / (levels * (levels + 1.0)) for k in range(levels)]
    for l in range(tiles):
        part = slice(l * BY, (l + 1) * BY)
        forcing = jnp.zeros((nrow, BY), F32)
        for i, (ref, coef) in enumerate(((st, -HEAT_COEF), (ss, SALT_COEF))):
            values = []
            for k in range(levels):
                right = ref[k, :, part]
                col = i * levels + k
                if l == tiles - 1:
                    right = right - jnp.where(lane == BY - 1, face_n[:, col : col + 1], 0.0)
                if l == 0:
                    right = right + jnp.where(lane == 0, face_s[:, col : col + 1], 0.0)
                if k > 0:
                    right = right + kv[k - 1, :, part] * values[k - 1]
                values.append(right * inv[k, :, part])
            x = values[levels - 1]
            ref[levels - 1, :, part] = x
            forcing = forcing + (coef * thick[levels - 1]) * x
            for k in range(levels - 2, -1, -1):
                x = values[k] + ratio[k, :, part] * x
                ref[k, :, part] = x
                forcing = forcing + (coef * thick[k]) * x
        src[:, part] = forcing

    second = [
        remote(src.at[pl.ds(nrow - 8, 8), :], src_w, send2, recv2, 0, (east, gy)),
        remote(src.at[pl.ds(0, 8), :], src_e, send2, recv2, 1, (west, gy)),
        remote(src.at[:, pl.ds(nlane - BY, BY)], src_s, send2, recv2, 2, (gx, north)),
        remote(src.at[:, pl.ds(0, BY)], src_n, send2, recv2, 3, (gx, south)),
    ] + [
        remote(corner_of(src, dx, dy), src_c.at[c], send2, recv2, 4 + c, (pick_x[dx], pick_y[dy]))
        for c, (dx, dy) in enumerate(CORNERS)
    ]
    for copy in second:
        copy.start()
    out_t = pltpu.make_async_copy(st, t_out, out_sem.at[0])
    out_s = pltpu.make_async_copy(ss, s_out, out_sem.at[1])
    out_t.start()
    out_s.start()

    sub8 = lax.broadcasted_iota(jnp.int32, (8, nlane), 0) < 4
    low_r = lane < BY // 2
    corner_lane = lax.broadcasted_iota(jnp.int32, (8, BY), 1) < BY // 2
    corner_sub = lax.broadcasted_iota(jnp.int32, (8, BY), 0) < 4

    def ring(centre, e, w, n, s, ne, se, nw, sw):
        rows = jnp.where(sub8, e, w)
        columns = jnp.where(low_r, n, s)
        corner = jnp.where(
            corner_sub, jnp.where(corner_lane, ne, se), jnp.where(corner_lane, nw, sw)
        )
        return jnp.concatenate(
            [
                jnp.concatenate([centre, columns], axis=1),
                jnp.concatenate([rows, corner], axis=1),
            ],
            axis=0,
        )

    wide = ring(
        layers,
        from_e[2 * levels :, :], from_w[3 * levels :, :],
        from_n[:, BY:] * ends_n, from_s[:, BY:] * ends_s,
        layer_c[3] * ends_n, layer_c[2] * ends_s, layer_c[1] * ends_n, layer_c[0] * ends_s,
    )
    depth = wide * (wide + 1.0) * (1.0 / (levels * (levels + 1.0)))
    bands_all = tiles * ny
    base = gy * tiles

    def flag(b):
        return jnp.where(table[lax.rem(b + bands_all, bands_all)] >= 0, 1.0, 0.0).astype(F32)

    full = (nrow + 8, BY)
    outer = lax.broadcasted_iota(jnp.int32, full, 1) < BY // 2
    flags = jnp.concatenate(
        [jnp.full(full, flag(base + l), F32) for l in range(tiles)]
        + [
            jnp.where(
                outer,
                jnp.full(full, flag(base + tiles), F32),
                jnp.full(full, flag(base - 1), F32),
            )
        ],
        axis=1,
    )
    ocean = jnp.where(depth > 0.0, flags, 0.0)
    pair = ocean * roll(ocean, -1, 0)
    deep = depth + roll(depth, -1, 0)
    quarter = (pair * roll(pair, -1, 1)) * (deep + roll(deep, -1, 1)) * (0.25 * 0.25)
    around = quarter + roll(quarter, 1, 0)
    around = around + roll(around, 1, 1)
    diagonal = ocean * (SURFACE_TERM + 6.0 * around)

    def operate(e):
        b = roll(e, -1, 0)
        c = roll(e, -1, 1)
        d = roll(b, -1, 1)
        p = e + d
        q = b + c
        total = p + q
        even = quarter * (total + q)
        odd = quarter * (total + p)
        spread = even + roll(odd, 1, 0) + roll(odd + roll(even, 1, 0), 1, 1)
        return diagonal * e - ocean * spread

    for copy in second:
        copy.wait_recv()
    residual = ocean * ring(
        src[...], src_e[...], src_w[...], src_n[...], src_s[...],
        src_c[3], src_c[2], src_c[1], src_c[0],
    )
    scaled = CENTER / HALF_SPAN
    direction = residual * (1.0 / CENTER)
    weight = 1.0 / scaled
    total = direction
    for _ in range(SWEEPS - 1):
        residual = residual - operate(direction)
        following = 1.0 / (2.0 * scaled - weight)
        direction = (following * weight) * direction + (2.0 * following / HALF_SPAN) * residual
        weight = following
        total = total + direction
    height[...] = total[:nrow, :nlane]
    for i in range(tiles):
        bands[i] = total[:nrow, i * BY : (i + 1) * BY]
    out_h = pltpu.make_async_copy(height, h_out, out_sem.at[2])
    out_h.start()

    def each(act_far, act_near=None):
        for i in range(tiles):
            b = base + i
            for m in range(reach):
                u = b // KB - m
                slot = lax.rem(b, KB) + KB * m
                peer = ny - 1 - u
                fits = (u >= 0) & (u < ny) & (slot < slots)

                @pl.when(fits & (peer != gy))
                def _():
                    act_far(
                        pltpu.make_async_remote_copy(
                            src_ref=bands.at[i], dst_ref=pool.at[slot],
                            send_sem=send3.at[i, m], recv_sem=recv3.at[slot],
                            device_id=(gx, peer), device_id_type=MESH,
                        )
                    )

                if act_near is None:
                    continue

                @pl.when(fits & (peer == gy))
                def _():
                    act_near(pltpu.make_async_copy(bands.at[i], pool.at[slot], recv3.at[slot]))

    each(lambda c: c.start(), lambda c: c.start())
    start = jnp.int32(0)
    for b in range(bands_all):
        start = start + jnp.where(table[b] == 0, b, 0)
    start = jnp.minimum(start, ny)
    for slot in range(slots):
        pltpu.make_async_copy(pool.at[slot], pool.at[slot], recv3.at[slot]).wait()
    for i in range(KB):
        block[:, i * BY : (i + 1) * BY] = reverse_lanes(pool[start + (KB - 1 - i)])
    out_b = pltpu.make_async_copy(block, b_out, out_sem.at[3])
    out_b.start()
    for copy in first + second:
        copy.wait_send()
    each(lambda c: c.wait_send())
    for copy in (out_t, out_s, out_h, out_b):
        copy.wait()


def body(nx, ny, t, s, u, v, k, layers, table):
    levels, nrow, nlane = t.shape
    tiles = nlane // BY
    reach = (ny + KB - 1) // KB + 1
    cube = pltpu.VMEM((levels, nrow, nlane), F32)
    lower = pltpu.VMEM((levels - 1, nrow, nlane), F32)
    plane = pltpu.VMEM((nrow, nlane), F32)
    side_y = pltpu.VMEM((nrow, BY), F32)
    side_x = pltpu.VMEM((8, nlane), F32)
    corners = pltpu.VMEM((4, 8, BY), F32)
    wide = pltpu.VMEM((3 * levels + 8, nlane), F32)
    slim = pltpu.VMEM((2 * levels + 8, nlane), F32)
    pair = pltpu.VMEM((nrow, 2 * BY), F32)
    dma = pltpu.SemaphoreType.DMA
    anywhere = pl.BlockSpec(memory_space=pl.ANY)
    return pl.pallas_call(
        functools.partial(kernel, nx, ny),
        out_shape=(
            jax.ShapeDtypeStruct(t.shape, F32),
            jax.ShapeDtypeStruct(t.shape, F32),
            jax.ShapeDtypeStruct((nrow, nlane), F32),
            jax.ShapeDtypeStruct((nrow, RB), F32),
        ),
        in_specs=[pl.BlockSpec(memory_space=pltpu.SMEM)] + [anywhere] * 6,
        out_specs=(anywhere,) * 4,
        scratch_shapes=[
            cube, cube, cube, cube, lower, pltpu.VMEM((nrow, nlane), jnp.int32), plane,
            cube, cube, cube, lower,
            wide, slim, pair, pair, wide, slim, pair, pair, corners,
            plane, side_x, side_x, side_y, side_y, corners,
            pltpu.VMEM((tiles, nrow, BY), F32), pltpu.VMEM((ny + KB, nrow, BY), F32),
            plane, pltpu.VMEM((nrow, RB), F32),
            dma((6,)), dma((4,)), dma((8,)), dma((8,)), dma((8,)), dma((8,)),
            dma((tiles, reach)), dma((ny + KB,)),
        ],
        compiler_params=pltpu.CompilerParams(
            collective_id=0, has_side_effects=True, vmem_limit_bytes=32 * 1024 * 1024
        ),
    )(table, t, s, u, v, k, layers)


def solution(mesh):
    cube = P(None, "gx", "gy")
    plane = P("gx", "gy")
    return jax.shard_map(
        functools.partial(body, mesh.shape["gx"], mesh.shape["gy"]),
        mesh=mesh,
        in_specs=(cube,) * 5 + (plane, P()),
        out_specs=(cube, cube, plane, plane),
        check_vma=False,
    )
```

time: 86.4 us -> 33.4 us (0.39)
  Pallas kernels: 0 us -> 22.9 us
  starting transfers between devices: 22.7 us -> 0 us
  blocking collectives: 17.4 us -> 0 us
  other arithmetic: 17.1 us -> 0 us
  waiting for transfers between devices: 12.4 us -> 0 us
  local copies, waits for them, and re-layouts: 13.9 us -> 9.51 us
  between operations: 2.33 us -> 0.66 us
    pallas_call x0 -> x1, Pallas kernels: none -> 22.9 us  [body(): pl.pallas_call(functools.partial(kernel, nx, ny), out_shape=(jax.ShapeDty...]
    ppermute x16 -> x0, starting transfers between devices: 22.7 us -> none  [the longest x8 18.2 us: padded_2(): lax.ppermute(lax.slice_in_dim(block, 0, width, axis=dim), axis, backward)]
    all_gather x3 -> x0, blocking collectives: 17.4 us -> none  [the longest x1 5.97 us: body(): lax.all_gather(depth_strip, 'gy', axis=1, tiled=True)]
    ppermute x16 -> x0, waiting for transfers between devices: 12.4 us -> none  [the longest x8 9.44 us: padded_2(): lax.ppermute(lax.slice_in_dim(block, block.shape[dim] - width, None, axis...]
    mul x11 -> x0, other arithmetic: 5.19 us -> none  [the longest x2 2.02 us: body(): wet_ext[:, :-1, 1:-1] * wet_ext[:, 1:, 1:-1]]
    concatenate x9 -> x0, other arithmetic: 2.46 us -> none  [the longest x8 2.46 us: padded_2(): block = jnp.concatenate([low, block, high], axis=dim)]
    reduce_sum x4 -> x0, other arithmetic: 2.05 us -> none  [the longest x1 1.17 us: body(): jnp.sum(thicknesses[:, None, None] * (SALT_COEF * mixed_columns[1] - HEAT...]
    rev x2 -> x0, local copies, waits for them, and re-layouts: 1.7 us -> none  [the longest x1 1.46 us: body(): surface = reversed_surface[:, ::-1]]
  transfers between devices with their start and end apart: 16 -> 0, of which waited for: 10 -> 0; matrix products, arithmetic and copies ran while one was open for 9% -> 0% of each run, Pallas kernels for 0% -> 0%
where the time goes in v1:
time: 33.4 us; the launch traced here: 33 us
  Pallas kernels  22.9 us (69%)
  local copies, waits for them, and re-layouts  9.51 us (28%)
  between operations  0.66 us (2%)
    pallas_call x1, Pallas kernels, body(): pl.pallas_call(functools.partial(kernel, nx, ny), out_shape=(jax.ShapeDty...  22.9 us
    unnamed x18, local copies, waits for them, and re-layouts  9.51 us

profile of v1, /device:TPU:0, one launch (start us, length us, event | category | flops | bytes accessed | tf_op | source)
XLA Modules:
  0.0 33.0 jit_solution(8609200364352220047)
XLA Ops:
  0.6 0.0 copy-start
  0.6 1.0 %copy-done = f32[8,32,512]{2,1,0:T(8,128)S(1)} copy-done((f32[8,32,512]{2,1,0:T(8,128)S(1)}, f32[8,32,512]{2,1,0:T(8,128)}, u32[]{:S(2)}) %copy-start) | copy-done | bytes 524312
  1.7 0.0 copy-start.1
  1.7 1.0 %copy-done.1 = f32[8,32,512]{2,1,0:T(8,128)S(1)} copy-done((f32[8,32,512]{2,1,0:T(8,128)S(1)}, f32[8,32,512]{2,1,0:T(8,128)}, u32[]{:S(2)}) %copy-start.1) | copy-done | bytes 524312
  2.7 0.0 copy-start.2
  2.7 1.0 %copy-done.2 = f32[8,32,512]{2,1,0:T(8,128)S(1)} copy-done((f32[8,32,512]{2,1,0:T(8,128)S(1)}, f32[8,32,512]{2,1,0:T(8,128)}, u32[]{:S(2)}) %copy-start.2) | copy-done | bytes 524312
  3.8 0.0 copy-start.3
  3.8 1.0 %copy-done.3 = f32[8,32,512]{2,1,0:T(8,128)S(1)} copy-done((f32[8,32,512]{2,1,0:T(8,128)S(1)}, f32[8,32,512]{2,1,0:T(8,128)}, u32[]{:S(2)}) %copy-start.3) | copy-done | bytes 524312
  4.8 0.0 copy-start.4
  4.8 1.0 %copy-done.4 = f32[7,32,512]{2,1,0:T(8,128)S(1)} copy-done((f32[7,32,512]{2,1,0:T(8,128)S(1)}, f32[7,32,512]{2,1,0:T(8,128)}, u32[]{:S(2)}) %copy-start.4) | copy-done | bytes 458776
  5.8 0.0 copy-start.5
  5.8 0.8 %copy-done.5 = s32[32,512]{1,0:T(8,128)S(1)} copy-done((s32[32,512]{1,0:T(8,128)S(1)}, s32[32,512]{1,0:T(8,128)}, u32[]{:S(2)}) %copy-start.5) | copy-done | bytes 65560
  6.7 0.0 copy-start.6
  6.7 0.7 %copy-done.6 = s32[16]{0:T(128)S(1)} copy-done((s32[16]{0:T(128)S(1)}, s32[16]{0:T(128)}, u32[]{:S(2)}) %copy-start.6) | copy-done | bytes 88
  7.3 22.9 %shard_map.102 = (f32[8,32,512]{2,1,0:T(8,128)S(1)}, f32[8,32,512]{2,1,0:T(8,128)S(1)}, f32[32,512]{1,0:T(8,128)S(1)}, f32[32,384]{1,0:T(8,128)S(1)}) custom-call(s32[16]{0:T(128)S(1)} %copy-done.6, f32[8,32,512]{2,1,0:T(8,128)S(1)} %copy-done, f32[8,32,512]{2,1,0:T(8,128)S(1)} %copy-done.1, f32[8,32,512]{2,1,0:T(8,128)S(1)} %copy-done.2, ...), custom_call_target="tpu_custom_call" | custom-call | tf_op jit(solution)/shard_map/pallas_call | solution.py:397
  30.2 0.8 %copy.15 = f32[8,32,512]{2,1,0:T(8,128)} copy(f32[8,32,512]{2,1,0:T(8,128)S(1)} %get-tuple-element.8) | data formatting | bytes 1048576
  31.0 0.8 %copy.16 = f32[8,32,512]{2,1,0:T(8,128)} copy(f32[8,32,512]{2,1,0:T(8,128)S(1)} %get-tuple-element.9) | data formatting | bytes 1048576
  31.8 0.6 %copy.17 = f32[32,512]{1,0:T(8,128)} copy(f32[32,512]{1,0:T(8,128)S(1)} %get-tuple-element.10) | data formatting | bytes 131072
  32.4 0.6 %copy.18 = f32[32,384]{1,0:T(8,128)} copy(f32[32,384]{1,0:T(8,128)S(1)} %get-tuple-element.11) | data formatting | bytes 98304
Async XLA Ops:
  0.6 1.0 %copy-start = (f32[8,32,512]{2,1,0:T(8,128)S(1)}, f32[8,32,512]{2,1,0:T(8,128)}, u32[]{:S(2)}) copy-start(f32[8,32,512]{2,1,0:T(8,128)} %t_hbm.1) | copy-start | bytes 1572868
  1.7 1.0 %copy-start.1 = (f32[8,32,512]{2,1,0:T(8,128)S(1)}, f32[8,32,512]{2,1,0:T(8,128)}, u32[]{:S(2)}) copy-start(f32[8,32,512]{2,1,0:T(8,128)} %s_hbm.1) | copy-start | bytes 1572868
  2.7 1.0 %copy-start.2 = (f32[8,32,512]{2,1,0:T(8,128)S(1)}, f32[8,32,512]{2,1,0:T(8,128)}, u32[]{:S(2)}) copy-start(f32[8,32,512]{2,1,0:T(8,128)} %u_hbm.1) | copy-start | bytes 1572868
  3.8 1.0 %copy-start.3 = (f32[8,32,512]{2,1,0:T(8,128)S(1)}, f32[8,32,512]{2,1,0:T(8,128)}, u32[]{:S(2)}) copy-start(f32[8,32,512]{2,1,0:T(8,128)} %v_hbm.1) | copy-start | bytes 1572868
  4.8 1.0 %copy-start.4 = (f32[7,32,512]{2,1,0:T(8,128)S(1)}, f32[7,32,512]{2,1,0:T(8,128)}, u32[]{:S(2)}) copy-start(f32[7,32,512]{2,1,0:T(8,128)} %k_hbm.1) | copy-start | bytes 1376260
  5.8 0.8 %copy-start.5 = (s32[32,512]{1,0:T(8,128)S(1)}, s32[32,512]{1,0:T(8,128)}, u32[]{:S(2)}) copy-start(s32[32,512]{1,0:T(8,128)} %l_hbm.1) | copy-start | bytes 196612
  6.7 0.7 %copy-start.6 = (s32[16]{0:T(128)S(1)}, s32[16]{0:T(128)}, u32[]{:S(2)}) copy-start(s32[16]{0:T(128)} %table.1) | copy-start | bytes 196

commit v2 on v1

--- a/solution.py
+++ b/solution.py
@@ -47,12 +47,12 @@
 
 def kernel(
     nx, ny, table, t_hbm, s_hbm, u_hbm, v_hbm, k_hbm, l_hbm,
-    t_out, s_out, h_out, b_out,
-    tv, sv, uv, vv, kv, lv, lf, st, ss, inv, ratio,
+    st, ss, height, block,
+    tv, sv, uv, vv, kv, lv, lf, inv, ratio,
     to_e, to_w, to_n, to_s, from_w, from_e, from_s, from_n, layer_c,
     src, src_w, src_e, src_s, src_n, src_c,
-    bands, pool, height, block,
-    in_sem, out_sem, send1, recv1, send2, recv2, send3, recv3,
+    bands, pool,
+    in_sem, send1, recv1, send2, recv2, send3, recv3,
 ):
     levels, nrow, nlane = t_hbm.shape
     tiles = nlane // BY
@@ -88,6 +88,7 @@
     lf[...] = lv[...].astype(F32)
     for copy in loads[1:5]:
         copy.wait()
+
 
     for k in range(levels):
         to_e[k : k + 1, :] = tv[k, nrow - 1 : nrow, :]
@@ -133,6 +134,7 @@
     ]
     for copy in first:
         copy.start()
+
 
     layers = lf[...]
     row_id = lax.broadcasted_iota(jnp.int32, (nrow, nlane), 0)
@@ -167,8 +169,9 @@
                 ratio[k, :, part] = last
                 below = above
 
-    for copy in first:
+    for copy in first[:4]:
         copy.wait_recv()
+
     ends_n = jnp.where(gy == ny - 1, 0.0, 1.0).astype(F32)
     ends_s = jnp.where(gy == 0, 0.0, 1.0).astype(F32)
 
@@ -232,6 +235,7 @@
                 forcing = forcing + (coef * thick[k]) * x
         src[:, part] = forcing
 
+
     second = [
         remote(src.at[pl.ds(nrow - 8, 8), :], src_w, send2, recv2, 0, (east, gy)),
         remote(src.at[pl.ds(0, 8), :], src_e, send2, recv2, 1, (west, gy)),
@@ -243,10 +247,6 @@
     ]
     for copy in second:
         copy.start()
-    out_t = pltpu.make_async_copy(st, t_out, out_sem.at[0])
-    out_s = pltpu.make_async_copy(ss, s_out, out_sem.at[1])
-    out_t.start()
-    out_s.start()
 
     sub8 = lax.broadcasted_iota(jnp.int32, (8, nlane), 0) < 4
     low_r = lane < BY // 2
@@ -267,6 +267,8 @@
             axis=0,
         )
 
+    for copy in first[4:]:
+        copy.wait_recv()
     wide = ring(
         layers,
         from_e[2 * levels :, :], from_w[3 * levels :, :],
@@ -315,6 +317,7 @@
 
     for copy in second:
         copy.wait_recv()
+
     residual = ocean * ring(
         src[...], src_e[...], src_w[...], src_n[...], src_s[...],
         src_c[3], src_c[2], src_c[1], src_c[0],
@@ -332,8 +335,7 @@
     height[...] = total[:nrow, :nlane]
     for i in range(tiles):
         bands[i] = total[:nrow, i * BY : (i + 1) * BY]
-    out_h = pltpu.make_async_copy(height, h_out, out_sem.at[2])
-    out_h.start()
+
 
     def each(act_far, act_near=None):
         for i in range(tiles):
@@ -370,12 +372,18 @@
         pltpu.make_async_copy(pool.at[slot], pool.at[slot], recv3.at[slot]).wait()
     for i in range(KB):
         block[:, i * BY : (i + 1) * BY] = reverse_lanes(pool[start + (KB - 1 - i)])
-    out_b = pltpu.make_async_copy(block, b_out, out_sem.at[3])
-    out_b.start()
     for copy in first + second:
         copy.wait_send()
     each(lambda c: c.wait_send())
-    for copy in (out_t, out_s, out_h, out_b):
+
+
+def write_out(*refs):
+    copies = [
+        pltpu.make_async_copy(refs[i], refs[4 + i], refs[8].at[i]) for i in range(4)
+    ]
+    for copy in copies:
+        copy.start()
+    for copy in copies:
         copy.wait()
 
 
@@ -394,30 +402,36 @@
     pair = pltpu.VMEM((nrow, 2 * BY), F32)
     dma = pltpu.SemaphoreType.DMA
     anywhere = pl.BlockSpec(memory_space=pl.ANY)
-    return pl.pallas_call(
+    held = pl.pallas_call(
         functools.partial(kernel, nx, ny),
         out_shape=(
-            jax.ShapeDtypeStruct(t.shape, F32),
-            jax.ShapeDtypeStruct(t.shape, F32),
-            jax.ShapeDtypeStruct((nrow, nlane), F32),
-            jax.ShapeDtypeStruct((nrow, RB), F32),
+            pltpu.VMEM(t.shape, F32),
+            pltpu.VMEM(t.shape, F32),
+            pltpu.VMEM((nrow, nlane), F32),
+            pltpu.VMEM((nrow, RB), F32),
         ),
         in_specs=[pl.BlockSpec(memory_space=pltpu.SMEM)] + [anywhere] * 6,
-        out_specs=(anywhere,) * 4,
+        out_specs=(pl.BlockSpec(memory_space=pltpu.VMEM),) * 4,
         scratch_shapes=[
             cube, cube, cube, cube, lower, pltpu.VMEM((nrow, nlane), jnp.int32), plane,
-            cube, cube, cube, lower,
+            cube, lower,
             wide, slim, pair, pair, wide, slim, pair, pair, corners,
             plane, side_x, side_x, side_y, side_y, corners,
             pltpu.VMEM((tiles, nrow, BY), F32), pltpu.VMEM((ny + KB, nrow, BY), F32),
-            plane, pltpu.VMEM((nrow, RB), F32),
-            dma((6,)), dma((4,)), dma((8,)), dma((8,)), dma((8,)), dma((8,)),
+            dma((6,)), dma((8,)), dma((8,)), dma((8,)), dma((8,)),
             dma((tiles, reach)), dma((ny + KB,)),
         ],
         compiler_params=pltpu.CompilerParams(
-            collective_id=0, has_side_effects=True, vmem_limit_bytes=32 * 1024 * 1024
+            collective_id=0, has_side_effects=True
         ),
     )(table, t, s, u, v, k, layers)
+    return pl.pallas_call(
+        write_out,
+        out_shape=tuple(jax.ShapeDtypeStruct(x.shape, F32) for x in held),
+        in_specs=[pl.BlockSpec(memory_space=pltpu.VMEM)] * 4,
+        out_specs=(pl.BlockSpec(memory_space=pltpu.HBM),) * 4,
+        scratch_shapes=[dma((4,))],
+    )(*[pltpu.with_memory_space_constraint(x, pltpu.VMEM) for x in held])
 
 
 def solution(mesh):

time: 33.4 us -> 24.4 us (0.73)
  local copies, waits for them, and re-layouts: 9.51 us -> 0 us
  Pallas kernels: 22.9 us -> 23.6 us
    unnamed x18 -> x0, local copies, waits for them, and re-layouts: 9.51 us -> none
    pallas_call x1 -> x2, Pallas kernels: 22.9 us -> 23.6 us  [the longest x1 22.5 us: body(): pl.pallas_call(functools.partial(kernel, nx, ny), out_shape=(pltpu.VMEM(t...]
where the time goes in v2:
time: 24.4 us; the launch traced here: 24.2 us
  Pallas kernels  23.6 us (97%)
  between operations  0.64 us (3%)
    pallas_call x1, Pallas kernels, body(): pl.pallas_call(functools.partial(kernel, nx, ny), out_shape=(pltpu.VMEM(t...  22.5 us
    pallas_call x1, Pallas kernels, body(): pl.pallas_call(write_out, out_shape=tuple((jax.ShapeDtypeStruct(x.shape,...  1.02 us

profile of v2, /device:TPU:0, one launch (start us, length us, event | category | flops | bytes accessed | tf_op | source)
XLA Modules:
  0.0 24.2 jit_solution(4455735505270357185)
XLA Ops:
  0.6 22.5 %shard_map.102 = (f32[8,32,512]{2,1,0:T(8,128)S(1)}, f32[8,32,512]{2,1,0:T(8,128)S(1)}, f32[32,512]{1,0:T(8,128)S(1)}, f32[32,384]{1,0:T(8,128)S(1)}) custom-call(s32[16]{0:T(128)} %table.1, f32[8,32,512]{2,1,0:T(8,128)} %t_hbm.1, f32[8,32,512]{2,1,0:T(8,128)} %s_hbm.1, f32[8,32,512]{2,1,0:T(8,128)} %u_hbm.1, f32[8,32,512]{2,1,0:T(8,128)} %v_hbm.1, ...), custom_call_target="tpu_custom_call" | custom-call | tf_op jit(solution)/shard_map/pallas_call | solution.py:405
  23.2 1.0 %shard_map.103 = (f32[8,32,512]{2,1,0:T(8,128)}, f32[8,32,512]{2,1,0:T(8,128)}, f32[32,512]{1,0:T(8,128)}, f32[32,384]{1,0:T(8,128)}) custom-call(f32[8,32,512]{2,1,0:T(8,128)S(1)} %get-tuple-element.8.refs_0_, f32[8,32,512]{2,1,0:T(8,128)S(1)} %get-tuple-element.9.refs_1_, f32[32,512]{1,0:T(8,128)S(1)} %get-tuple-element.10.refs_2_, ...), custom_call_target="tpu_custom_call" | custom-call | tf_op jit(solution)/shard_map/pallas_call | solution.py:428
